TPU v7x, 32 devices: a whole 2x2x4 slice. The times are simulated.
32 devices in a mesh: gx: 8 (over z, x), gy: 4 (over y, core).
Axes of the slice: x: 2, y: 2, z: 4, core: 2. Of those that a mesh axis runs over, the one named last changes fastest.
Arguments:
- rhs_field: float32 [64, 32, 128], P('gx', 'gy'), may hold values from -6 to 6
- accumulation: float32 [64, 32, 128], P('gx', 'gy'), may hold values from 0.05 to 0.5
- trans_x: float32 [64, 32, 128], P('gx', 'gy'), may hold values from 0.1 to 10
- trans_y: float32 [64, 32, 128], P('gx', 'gy'), may hold values from 0.1 to 10
- trans_z: float32 [64, 32, 128], P('gx', 'gy'), may hold values from 0.02 to 2
- held_cells: int32 [4, 8, 8, 128], P(None, 'gx', 'gy'), may hold values from 0 to 8191
- perf_host: int32 [8, 8, 128], P('gx', 'gy'), may hold values from 0 to 3, as said below
- well_index: float32 [8, 8, 128], P('gx', 'gy'), may hold values from 0.1 to 2
- seg_cond: float32 [8, 8, 128], P('gx', 'gy'), may hold values from 0.5 to 4
- seg_rate: float32 [8, 8, 128], P('gx', 'gy'), may hold values from -6 to 6
Outputs:
- pressure: float32 [64, 32, 128], P('gx', 'gy')
- seg_pressure: float32 [8, 8, 128], P('gx', 'gy')
Inputs may be any that keep to these rules, and one draw needn't show every extreme that they name: `held_cells`: local cell numbers, x-major then y then layer. `perf_host`: nondecreasing along a well's slots, starting at 0 in slot 0 and ending at 3 in the last slot: the perforations on each device form one run of slots.
All inputs are finite; a program needn't handle non-finite values.
Results may differ from a plain program's by a relative error of at most 0.00002.
Values sent between devices are 32-bit elements; how exact they have to be, the bound alone decides.
A program may use at most 64 MiB of HBM per device.

v0:
```python
import functools

import jax
import jax.numpy as jnp
from jax import lax
from jax.experimental import pallas as pl
from jax.experimental.pallas import tpu as pltpu
from jax.sharding import PartitionSpec as P

SWEEPS = 6
MESH = pl.DeviceIdType.MESH
WEST, EAST, SOUTH, NORTH = range(4)
C_W, C_E, C_S, C_N, C_EDGE, C_D, C_U, C_INV, C_RHS = range(9)


def kernel(
    reach,
    rhs_ref,
    acc_ref,
    tx_ref,
    ty_ref,
    tz_ref,
    held_ref,
    host_ref,
    wi_ref,
    sc_ref,
    sr_ref,
    p_out,
    s_out,
    p_buf,
    halo,
    y_stage,
    coef,
    tx_halo,
    ty_halo,
    ty_stage,
    packs,
    params,
    held_buf,
    slot_z,
    seg_buf,
    seg_recv,
    init_send,
    init_recv,
    halo_send,
    halo_recv,
    seg_send,
    seg_rsem,
):
    cx, cy, cz = rhs_ref.shape
    wells = wi_ref.shape[1]
    rows = reach * wells
    gx, gy = lax.axis_index("gx"), lax.axis_index("gy")
    nx, ny = lax.axis_size("gx"), lax.axis_size("gy")
    has_w, has_e = gx > 0, gx < nx - 1
    has_s, has_n = gy > 0, gy < ny - 1
    offsets = [d for d in range(1 - reach, reach) if d != 0]
    index_of = {d: i for i, d in enumerate(offsets)}

    def along_x(d):
        return {"gx": lax.rem(gx + d + nx, nx)}

    def send(src, dst, ssem, rsem, device):
        return pltpu.make_async_remote_copy(
            src_ref=src,
            dst_ref=dst,
            send_sem=ssem,
            recv_sem=rsem,
            device_id=device,
            device_id_type=MESH,
        )

    zero = jnp.zeros((cy, cz), jnp.float32)
    for t in range(SWEEPS):
        for side in range(4):
            halo[t, side] = zero
    tx_halo[...] = zero
    ty_halo[...] = zero

    barrier = pltpu.get_barrier_semaphore()
    for d in offsets:
        pl.semaphore_signal(barrier, inc=1, device_id=along_x(d), device_id_type=MESH)

    @pl.when(has_s)
    def _():
        pl.semaphore_signal(barrier, inc=1, device_id={"gy": gy - 1}, device_id_type=MESH)

    @pl.when(has_n)
    def _():
        pl.semaphore_signal(barrier, inc=1, device_id={"gy": gy + 1}, device_id_type=MESH)

    packs[0, 0:wells] = host_ref[0].astype(jnp.float32)
    packs[0, wells : 2 * wells] = wi_ref[0]
    packs[0, 2 * wells : 3 * wells] = sc_ref[0]
    packs[0, 3 * wells : 4 * wells] = sr_ref[0]
    ty_stage[...] = ty_ref[:, cy - 1, :]
    pl.semaphore_wait(
        barrier, len(offsets) + has_s.astype(jnp.int32) + has_n.astype(jnp.int32)
    )

    def pack_copy(d):
        return send(
            packs.at[0], packs.at[d], init_send.at[d], init_recv.at[d], along_x(d)
        )

    def tx_copy():
        return send(
            tx_ref.at[cx - 1], tx_halo, init_send.at[0], init_recv.at[0], along_x(1)
        )

    def ty_copy():
        return send(
            ty_stage, ty_halo, init_send.at[reach], init_recv.at[reach], {"gy": gy + 1}
        )

    for d in range(reach - 1, 0, -1):
        pack_copy(d).start()
    pl.when(has_e)(lambda: tx_copy().start())
    pl.when(has_n)(lambda: ty_copy().start())

    for r in range(reach):
        held_buf[r * wells : (r + 1) * wells] = held_ref[r, 0]
    held = held_buf[...]
    row_of = held // cz
    z_of = held - row_of * cz
    z_iota = lax.broadcasted_iota(jnp.int32, (cz, cz), 0)
    for s in range(rows):
        hit = (z_iota == jnp.broadcast_to(z_of[s : s + 1, :], (cz, cz))).astype(jnp.float32)
        slot_z[s * cz : (s + 1) * cz, :] = hit.T.astype(jnp.bfloat16)
    row_iota = lax.broadcasted_iota(jnp.int32, (cx * cy, cz), 0)

    lane = lax.broadcasted_iota(jnp.int32, (cy, cz), 1)
    sub = lax.broadcasted_iota(jnp.int32, (cy, cz), 0)
    level = (lax.broadcasted_iota(jnp.int32, (rows, cz), 0) // wells).astype(jnp.float32)

    for d in range(1, reach):
        pack_copy(d).wait_recv()
    for r in range(reach):
        for k in range(4):
            params[k, r * wells : (r + 1) * wells] = packs[r, k * wells : (k + 1) * wells]
    host = params[0]
    wi = params[1]
    rate = params[3]
    slot = lax.broadcasted_iota(jnp.int32, (rows, cz), 1)
    fm = jnp.where(slot > 0, params[2], 0.0)
    fp = jnp.where(slot < cz - 1, pltpu.roll(fm, cz - 1, 1), 0.0)
    seg_inv = 0.8 / (wi + fm + fp)
    mine = host == level

    def gather(t):
        cell_p = jnp.zeros((rows, cz), jnp.float32)
        for x in range(cx):
            for y in range(cy):
                line = jnp.broadcast_to(p_buf[t, x, pl.ds(y, 1), :], (rows, cz))
                got = jnp.take_along_axis(line, z_of, axis=1, mode="promise_in_bounds")
                cell_p = jnp.where(row_of == x * cy + y, got, cell_p)
        return cell_p

    def scatter(flux):
        high = flux.astype(jnp.bfloat16).astype(jnp.float32)
        rest = flux - high
        mid = rest.astype(jnp.bfloat16).astype(jnp.float32)
        low = rest - mid
        parts = []
        for part in (high, mid, low):
            pieces = []
            for s in range(rows):
                at_row = row_iota == jnp.broadcast_to(row_of[s : s + 1, :], row_iota.shape)
                pieces.append(
                    jnp.where(at_row, jnp.broadcast_to(part[s : s + 1, :], row_iota.shape), 0.0)
                )
            parts.append(jnp.concatenate(pieces, axis=1).astype(jnp.bfloat16))
        spread = jnp.dot(
            jnp.concatenate(parts, axis=0), slot_z[...], preferred_element_type=jnp.float32
        )
        cells = cx * cy
        return spread[:cells] + spread[cells : 2 * cells] + spread[2 * cells :]

    def halo_copies(t):
        return (
            (has_w, send(p_buf.at[t, 0], halo.at[t, EAST], halo_send.at[t, WEST],
                         halo_recv.at[t, EAST], {"gx": gx - 1})),
            (has_e, send(p_buf.at[t, cx - 1], halo.at[t, WEST], halo_send.at[t, EAST],
                         halo_recv.at[t, WEST], {"gx": gx + 1})),
            (has_s, send(y_stage.at[t, 0], halo.at[t, NORTH], halo_send.at[t, SOUTH],
                         halo_recv.at[t, NORTH], {"gy": gy - 1})),
            (has_n, send(y_stage.at[t, 1], halo.at[t, SOUTH], halo_send.at[t, NORTH],
                         halo_recv.at[t, SOUTH], {"gy": gy + 1})),
        )

    def send_halos(t):
        y_stage[t, 0] = p_buf[t, :, 0, :]
        y_stage[t, 1] = p_buf[t, :, cy - 1, :]
        for there, copy in halo_copies(t):
            pl.when(there)(copy.start)

    def wait_halos(t):
        for there, slot_at in ((has_w, WEST), (has_e, EAST), (has_s, SOUTH), (has_n, NORTH)):
            copy = send(halo.at[t, slot_at], halo.at[t, slot_at], halo_send.at[t, slot_at],
                        halo_recv.at[t, slot_at], along_x(1))
            pl.when(there)(copy.wait_recv)

    def seg_copy(t, d):
        return send(seg_buf.at[t], seg_recv.at[t, index_of[-d]],
                    seg_send.at[t, index_of[d]], seg_rsem.at[t, index_of[-d]], along_x(d))

    def merge(t, seg):
        for d in offsets:
            seg_copy(t, d).wait_recv()
        for d in offsets:
            got = seg_recv[t, index_of[d]]
            got = pltpu.roll(got, (-d * wells) % rows, 0)
            seg = jnp.where(host == level + d, got, seg)
        return seg

    def well_step(t, seg, cell_p):
        before = pltpu.roll(seg, 1, 1)
        after = pltpu.roll(seg, cz - 1, 1)
        seg = 0.2 * seg + seg_inv * (rate + wi * cell_p + fm * before + fp * after)
        seg_buf[t] = seg
        for d in offsets:
            seg_copy(t, d).start()
        return seg

    def grid_step(t, well_term, result, at):
        parts = []
        for x in range(cx):
            p = p_buf[t, x]
            total = 0.3 * p + coef[C_RHS, x] - coef[C_INV, x] * well_term[x * cy : (x + 1) * cy]
            total += coef[C_U, x] * pltpu.roll(p, cz - 1, 1) + coef[C_D, x] * pltpu.roll(p, 1, 1)
            total += coef[C_N, x] * pltpu.roll(p, cy - 1, 0) + coef[C_S, x] * pltpu.roll(p, 1, 0)
            if x > 0:
                total += coef[C_W, x] * p_buf[t, x - 1]
            if x < cx - 1:
                total += coef[C_E, x] * p_buf[t, x + 1]
            parts.append(total)
        wait_halos(t)
        parts[0] += coef[C_W, 0] * halo[t, WEST]
        parts[-1] += coef[C_E, cx - 1] * halo[t, EAST]
        for x in range(cx):
            north = jnp.broadcast_to(halo[t, NORTH, pl.ds(x, 1), :], (cy, cz))
            south = jnp.broadcast_to(halo[t, SOUTH, pl.ds(x, 1), :], (cy, cz))
            edge = jnp.where(sub == 0, south, north)
            value = parts[x] + coef[C_EDGE, x] * edge
            if at is None:
                result[x] = value
            else:
                result[at, x] = value

    seg = seg_inv * rate
    well_term = scatter(jnp.where(mine, -wi * seg, 0.0))

    pl.when(has_w)(tx_copy().wait_recv)
    pl.when(has_s)(ty_copy().wait_recv)
    for x in range(cx):
        ex, ey, ez = tx_ref[x], ty_ref[x], tz_ref[x]
        wx = tx_halo[...] if x == 0 else tx_ref[x - 1]
        edge_y = jnp.broadcast_to(ty_halo[pl.ds(x, 1), :], (cy, cz))
        wy = jnp.where(sub == 0, edge_y, pltpu.roll(ey, 1, 0))
        wz = jnp.where(lane == 0, 0.0, pltpu.roll(ez, 1, 1))
        diag = acc_ref[x] + ex + wx + ey + wy + ez + wz
        inv = 0.7 / diag
        coef[C_W, x] = inv * wx
        coef[C_E, x] = inv * ex
        coef[C_S, x] = jnp.where(sub == 0, 0.0, inv * wy)
        coef[C_N, x] = jnp.where(sub == cy - 1, 0.0, inv * ey)
        coef[C_EDGE, x] = jnp.where(
            sub == 0, inv * wy, jnp.where(sub == cy - 1, inv * ey, 0.0)
        )
        coef[C_D, x] = inv * wz
        coef[C_U, x] = jnp.where(lane == cz - 1, 0.0, inv * ez)
        coef[C_INV, x] = inv
        right = inv * rhs_ref[x]
        coef[C_RHS, x] = right
        p_buf[1, x] = right - inv * well_term[x * cy : (x + 1) * cy]
    send_halos(1)

    def sweep(t, seg, first):
        cell_p = gather(t)
        if not first:
            seg = merge(t - 1, seg)
        seg = well_step(t, seg, cell_p)
        well_term = scatter(jnp.where(mine, wi * (cell_p - seg), 0.0))
        return seg, well_term

    def middle(t, seg, first):
        seg, well_term = sweep(t, seg, first)
        grid_step(t, well_term, p_buf, t + 1)
        send_halos(t + 1)
        return seg

    seg = middle(1, seg, True)
    seg = lax.fori_loop(2, SWEEPS - 1, lambda t, seg: middle(t, seg, False), seg)
    last = SWEEPS - 1
    seg, well_term = sweep(last, seg, False)
    grid_step(last, well_term, p_out, None)
    seg = merge(last, seg)
    s_out[0] = seg[:wells]

    for d in range(1, reach):
        pack_copy(d).wait_send()
    pl.when(has_e)(lambda: tx_copy().wait_send())
    pl.when(has_n)(lambda: ty_copy().wait_send())

    def drain(t, carry):
        for there, copy in halo_copies(t):
            pl.when(there)(copy.wait_send)
        for d in offsets:
            seg_copy(t, d).wait_send()
        return carry

    lax.fori_loop(1, SWEEPS, drain, 0)


def shards(rhs, acc, tx, ty, tz, held, host, wi, sc, sr):
    reach = held.shape[0]
    wells, slots = wi.shape[1:]
    rows = reach * wells
    cx, cy, cz = rhs.shape
    peers = 2 * (reach - 1)
    vmem = pl.BlockSpec(memory_space=pltpu.VMEM)
    f32 = jnp.float32
    return pl.pallas_call(
        functools.partial(kernel, reach),
        out_shape=(
            jax.ShapeDtypeStruct(rhs.shape, f32),
            jax.ShapeDtypeStruct(sr.shape, f32),
        ),
        in_specs=[vmem] * 10,
        out_specs=(vmem, vmem),
        scratch_shapes=[
            pltpu.VMEM((SWEEPS, cx, cy, cz), f32),
            pltpu.VMEM((SWEEPS, 4, cy, cz), f32),
            pltpu.VMEM((SWEEPS, 2, cx, cz), f32),
            pltpu.VMEM((9, cx, cy, cz), f32),
            pltpu.VMEM((cy, cz), f32),
            pltpu.VMEM((cx, cz), f32),
            pltpu.VMEM((cx, cz), f32),
            pltpu.VMEM((reach, 4 * wells, slots), f32),
            pltpu.VMEM((4, rows, slots), f32),
            pltpu.VMEM((rows, slots), jnp.int32),
            pltpu.VMEM((rows * slots, cz), jnp.bfloat16),
            pltpu.VMEM((SWEEPS, rows, slots), f32),
            pltpu.VMEM((SWEEPS, peers, rows, slots), f32),
            pltpu.SemaphoreType.DMA((reach + 1,)),
            pltpu.SemaphoreType.DMA((reach + 1,)),
            pltpu.SemaphoreType.DMA((SWEEPS, 4)),
            pltpu.SemaphoreType.DMA((SWEEPS, 4)),
            pltpu.SemaphoreType.DMA((SWEEPS, peers)),
            pltpu.SemaphoreType.DMA((SWEEPS, peers)),
        ],
        compiler_params=pltpu.CompilerParams(
            collective_id=0, has_side_effects=True, vmem_limit_bytes=32 * 1024 * 1024
        ),
    )(rhs, acc, tx, ty, tz, held, host, wi, sc, sr)


def solution(mesh):
    return jax.shard_map(
        shards,
        mesh=mesh,
        in_specs=(P("gx", "gy", None),) * 5
        + (P(None, "gx", "gy", None),)
        + (P("gx", "gy", None),) * 4,
        out_specs=(P("gx", "gy", None), P("gx", "gy", None)),
        check_vma=False,
    )
```

profile of v0, /device:TPU:0, one launch (start us, length us, event | category | flops | bytes accessed | tf_op | source)
XLA Modules:
  0.0 39.6 jit_solution(10226752731969239079)
XLA Ops:
  0.6 0.0 copy-start
  0.6 0.7 %copy-done = f32[8,8,128]{2,1,0:T(8,128)S(1)} copy-done((f32[8,8,128]{2,1,0:T(8,128)S(1)}, f32[8,8,128]{2,1,0:T(8,128)}, u32[]{:S(2)}) %copy-start) | copy-done | bytes 32792
  1.4 0.0 copy-start.1
  1.4 0.8 %copy-done.1 = f32[8,8,128]{2,1,0:T(8,128)S(1)} copy-done((f32[8,8,128]{2,1,0:T(8,128)S(1)}, f32[8,8,128]{2,1,0:T(8,128)}, u32[]{:S(2)}) %copy-start.1) | copy-done | bytes 32792
  2.2 0.0 copy-start.2
  2.2 0.8 %copy-done.2 = f32[8,8,128]{2,1,0:T(8,128)S(1)} copy-done((f32[8,8,128]{2,1,0:T(8,128)S(1)}, f32[8,8,128]{2,1,0:T(8,128)}, u32[]{:S(2)}) %copy-start.2) | copy-done | bytes 32792
  2.9 0.0 copy-start.3
  2.9 0.8 %copy-done.3 = f32[8,8,128]{2,1,0:T(8,128)S(1)} copy-done((f32[8,8,128]{2,1,0:T(8,128)S(1)}, f32[8,8,128]{2,1,0:T(8,128)}, u32[]{:S(2)}) %copy-start.3) | copy-done | bytes 32792
  3.7 0.0 copy-start.4
  3.7 0.8 %copy-done.4 = f32[8,8,128]{2,1,0:T(8,128)S(1)} copy-done((f32[8,8,128]{2,1,0:T(8,128)S(1)}, f32[8,8,128]{2,1,0:T(8,128)}, u32[]{:S(2)}) %copy-start.4) | copy-done | bytes 32792
  4.4 0.0 copy-start.5
  4.4 0.7 %copy-done.5 = s32[4,1,2,128]{3,2,1,0:T(2,128)S(1)} copy-done((s32[4,1,2,128]{3,2,1,0:T(2,128)S(1)}, s32[4,1,2,128]{3,2,1,0:T(2,128)}, u32[]{:S(2)}) %copy-start.5) | copy-done | bytes 4120
  5.1 0.0 copy-start.6
  5.1 0.7 %copy-done.6 = s32[1,2,128]{2,1,0:T(2,128)S(1)} copy-done((s32[1,2,128]{2,1,0:T(2,128)S(1)}, s32[1,2,128]{2,1,0:T(2,128)}, u32[]{:S(2)}) %copy-start.6) | copy-done | bytes 1048
  5.8 0.0 copy-start.7
  5.8 0.7 %copy-done.7 = f32[1,2,128]{2,1,0:T(2,128)S(1)} copy-done((f32[1,2,128]{2,1,0:T(2,128)S(1)}, f32[1,2,128]{2,1,0:T(2,128)}, u32[]{:S(2)}) %copy-start.7) | copy-done | bytes 1048
  6.5 0.0 copy-start.8
  6.5 0.7 %copy-done.8 = f32[1,2,128]{2,1,0:T(2,128)S(1)} copy-done((f32[1,2,128]{2,1,0:T(2,128)S(1)}, f32[1,2,128]{2,1,0:T(2,128)}, u32[]{:S(2)}) %copy-start.8) | copy-done | bytes 1048
  7.2 0.0 copy-start.9
  7.2 0.7 %copy-done.9 = f32[1,2,128]{2,1,0:T(2,128)S(1)} copy-done((f32[1,2,128]{2,1,0:T(2,128)S(1)}, f32[1,2,128]{2,1,0:T(2,128)}, u32[]{:S(2)}) %copy-start.9) | copy-done | bytes 1048
  7.8 30.6 %shard_map.113 = (f32[8,8,128]{2,1,0:T(8,128)S(1)}, f32[1,2,128]{2,1,0:T(2,128)S(1)}) custom-call(f32[8,8,128]{2,1,0:T(8,128)S(1)} %copy-done, f32[8,8,128]{2,1,0:T(8,128)S(1)} %copy-done.1, f32[8,8,128]{2,1,0:T(8,128)S(1)} %copy-done.2, f32[8,8,128]{2,1,0:T(8,128)S(1)} %copy-done.3, f32[8,8,128]{2,1,0:T(8,128)S(1)} %copy-done.4, ...), custom_call_target="tpu_custom_call" | custom-call | tf_op jit(solution)/shard_map/pallas_call | solution.py:323
  38.4 0.6 %copy.14 = f32[8,8,128]{2,1,0:T(8,128)} copy(f32[8,8,128]{2,1,0:T(8,128)S(1)} %get-tuple-element.4) | data formatting | bytes 65536
  39.0 0.6 %copy.15 = f32[1,2,128]{2,1,0:T(2,128)} copy(f32[1,2,128]{2,1,0:T(2,128)S(1)} %get-tuple-element.5) | data formatting | bytes 2048
Async XLA Ops:
  0.6 0.8 %copy-start = (f32[8,8,128]{2,1,0:T(8,128)S(1)}, f32[8,8,128]{2,1,0:T(8,128)}, u32[]{:S(2)}) copy-start(f32[8,8,128]{2,1,0:T(8,128)} %rhs_ref.1) | copy-start | bytes 98308
  1.4 0.8 %copy-start.1 = (f32[8,8,128]{2,1,0:T(8,128)S(1)}, f32[8,8,128]{2,1,0:T(8,128)}, u32[]{:S(2)}) copy-start(f32[8,8,128]{2,1,0:T(8,128)} %acc_ref.1) | copy-start | bytes 98308
  2.2 0.8 %copy-start.2 = (f32[8,8,128]{2,1,0:T(8,128)S(1)}, f32[8,8,128]{2,1,0:T(8,128)}, u32[]{:S(2)}) copy-start(f32[8,8,128]{2,1,0:T(8,128)} %tx_ref.1) | copy-start | bytes 98308
  2.9 0.8 %copy-start.3 = (f32[8,8,128]{2,1,0:T(8,128)S(1)}, f32[8,8,128]{2,1,0:T(8,128)}, u32[]{:S(2)}) copy-start(f32[8,8,128]{2,1,0:T(8,128)} %ty_ref.1) | copy-start | bytes 98308
  3.7 0.8 %copy-start.4 = (f32[8,8,128]{2,1,0:T(8,128)S(1)}, f32[8,8,128]{2,1,0:T(8,128)}, u32[]{:S(2)}) copy-start(f32[8,8,128]{2,1,0:T(8,128)} %tz_ref.1) | copy-start | bytes 98308
  4.4 0.7 %copy-start.5 = (s32[4,1,2,128]{3,2,1,0:T(2,128)S(1)}, s32[4,1,2,128]{3,2,1,0:T(2,128)}, u32[]{:S(2)}) copy-start(s32[4,1,2,128]{3,2,1,0:T(2,128)} %held_ref.1) | copy-start | bytes 12292
  5.1 0.7 %copy-start.6 = (s32[1,2,128]{2,1,0:T(2,128)S(1)}, s32[1,2,128]{2,1,0:T(2,128)}, u32[]{:S(2)}) copy-start(s32[1,2,128]{2,1,0:T(2,128)} %host_ref.1) | copy-start | bytes 3076
  5.8 0.7 %copy-start.7 = (f32[1,2,128]{2,1,0:T(2,128)S(1)}, f32[1,2,128]{2,1,0:T(2,128)}, u32[]{:S(2)}) copy-start(f32[1,2,128]{2,1,0:T(2,128)} %wi_ref.1) | copy-start | bytes 3076
  6.5 0.7 %copy-start.8 = (f32[1,2,128]{2,1,0:T(2,128)S(1)}, f32[1,2,128]{2,1,0:T(2,128)}, u32[]{:S(2)}) copy-start(f32[1,2,128]{2,1,0:T(2,128)} %sc_ref.1) | copy-start | bytes 3076
  7.2 0.7 %copy-start.9 = (f32[1,2,128]{2,1,0:T(2,128)S(1)}, f32[1,2,128]{2,1,0:T(2,128)}, u32[]{:S(2)}) copy-start(f32[1,2,128]{2,1,0:T(2,128)} %sr_ref.1) | copy-start | bytes 3076
where the time goes:
time: 40.2 us; the launch traced here: 39.6 us
  Pallas kernels  30.6 us (76%)
  local copies, waits for them, and re-layouts  8.36 us (21%)
  between operations  0.66 us (2%)
    pallas_call x1, Pallas kernels, shards(): pl.pallas_call(functools.partial(kernel, reach), out_shape=(jax.ShapeDtyp...  30.6 us
    unnamed x22, local copies, waits for them, and re-layouts  8.36 us

commit v1 on v0

--- a/solution.py
+++ b/solution.py
@@ -15,6 +15,18 @@
 
 def kernel(
     reach,
+    rhs_hbm,
+    acc_hbm,
+    tx_hbm,
+    ty_hbm,
+    tz_hbm,
+    held_hbm,
+    host_hbm,
+    wi_hbm,
+    sc_hbm,
+    sr_hbm,
+    p_out,
+    s_out,
     rhs_ref,
     acc_ref,
     tx_ref,
@@ -25,8 +37,7 @@
     wi_ref,
     sc_ref,
     sr_ref,
-    p_out,
-    s_out,
+    fetch_sem,
     p_buf,
     halo,
     y_stage,
@@ -38,14 +49,14 @@
     params,
     held_buf,
     slot_z,
-    seg_buf,
-    seg_recv,
+    cell_buf,
+    cell_recv,
     init_send,
     init_recv,
     halo_send,
     halo_recv,
-    seg_send,
-    seg_rsem,
+    cell_send,
+    cell_rsem,
 ):
     cx, cy, cz = rhs_ref.shape
     wells = wi_ref.shape[1]
@@ -89,6 +100,27 @@
     def _():
         pl.semaphore_signal(barrier, inc=1, device_id={"gy": gy + 1}, device_id_type=MESH)
 
+    fetches = [
+        pltpu.make_async_copy(src, dst, fetch_sem.at[i])
+        for i, (src, dst) in enumerate(
+            (
+                (host_hbm, host_ref),
+                (wi_hbm, wi_ref),
+                (sc_hbm, sc_ref),
+                (sr_hbm, sr_ref),
+                (ty_hbm, ty_ref),
+                (tx_hbm, tx_ref),
+                (held_hbm, held_ref),
+                (acc_hbm, acc_ref),
+                (tz_hbm, tz_ref),
+                (rhs_hbm, rhs_ref),
+            )
+        )
+    ]
+    for fetch in fetches:
+        fetch.start()
+    for fetch in fetches[:6]:
+        fetch.wait()
     packs[0, 0:wells] = host_ref[0].astype(jnp.float32)
     packs[0, wells : 2 * wells] = wi_ref[0]
     packs[0, 2 * wells : 3 * wells] = sc_ref[0]
@@ -117,6 +149,9 @@
         pack_copy(d).start()
     pl.when(has_e)(lambda: tx_copy().start())
     pl.when(has_n)(lambda: ty_copy().start())
+
+    for fetch in fetches[6:]:
+        fetch.wait()
 
     for r in range(reach):
         held_buf[r * wells : (r + 1) * wells] = held_ref[r, 0]
@@ -133,28 +168,18 @@
     sub = lax.broadcasted_iota(jnp.int32, (cy, cz), 0)
     level = (lax.broadcasted_iota(jnp.int32, (rows, cz), 0) // wells).astype(jnp.float32)
 
-    for d in range(1, reach):
-        pack_copy(d).wait_recv()
-    for r in range(reach):
-        for k in range(4):
-            params[k, r * wells : (r + 1) * wells] = packs[r, k * wells : (k + 1) * wells]
-    host = params[0]
-    wi = params[1]
-    rate = params[3]
-    slot = lax.broadcasted_iota(jnp.int32, (rows, cz), 1)
-    fm = jnp.where(slot > 0, params[2], 0.0)
-    fp = jnp.where(slot < cz - 1, pltpu.roll(fm, cz - 1, 1), 0.0)
-    seg_inv = 0.8 / (wi + fm + fp)
-    mine = host == level
-
     def gather(t):
-        cell_p = jnp.zeros((rows, cz), jnp.float32)
+        found = []
         for x in range(cx):
+            cell_p = jnp.zeros((rows, cz), jnp.float32)
             for y in range(cy):
                 line = jnp.broadcast_to(p_buf[t, x, pl.ds(y, 1), :], (rows, cz))
                 got = jnp.take_along_axis(line, z_of, axis=1, mode="promise_in_bounds")
                 cell_p = jnp.where(row_of == x * cy + y, got, cell_p)
-        return cell_p
+            found.append(cell_p)
+        while len(found) > 1:
+            found = [sum(found[i : i + 2]) for i in range(0, len(found), 2)]
+        return found[0]
 
     def scatter(flux):
         high = flux.astype(jnp.bfloat16).astype(jnp.float32)
@@ -200,27 +225,23 @@
                         halo_recv.at[t, slot_at], along_x(1))
             pl.when(there)(copy.wait_recv)
 
-    def seg_copy(t, d):
-        return send(seg_buf.at[t], seg_recv.at[t, index_of[-d]],
-                    seg_send.at[t, index_of[d]], seg_rsem.at[t, index_of[-d]], along_x(d))
-
-    def merge(t, seg):
+    def cell_copy(t, d):
+        return send(cell_buf.at[t], cell_recv.at[t, index_of[-d]],
+                    cell_send.at[t, index_of[d]], cell_rsem.at[t, index_of[-d]], along_x(d))
+
+    def merge(t):
+        cell_p = cell_buf[t]
         for d in offsets:
-            seg_copy(t, d).wait_recv()
+            cell_copy(t, d).wait_recv()
         for d in offsets:
-            got = seg_recv[t, index_of[d]]
-            got = pltpu.roll(got, (-d * wells) % rows, 0)
-            seg = jnp.where(host == level + d, got, seg)
-        return seg
-
-    def well_step(t, seg, cell_p):
+            got = pltpu.roll(cell_recv[t, index_of[d]], (-d * wells) % rows, 0)
+            cell_p = jnp.where(host == level + d, got, cell_p)
+        return cell_p
+
+    def well_step(seg, cell_p):
         before = pltpu.roll(seg, 1, 1)
         after = pltpu.roll(seg, cz - 1, 1)
-        seg = 0.2 * seg + seg_inv * (rate + wi * cell_p + fm * before + fp * after)
-        seg_buf[t] = seg
-        for d in offsets:
-            seg_copy(t, d).start()
-        return seg
+        return 0.2 * seg + seg_inv * (rate + wi * cell_p + fm * before + fp * after)
 
     def grid_step(t, well_term, result, at):
         parts = []
@@ -247,9 +268,6 @@
             else:
                 result[at, x] = value
 
-    seg = seg_inv * rate
-    well_term = scatter(jnp.where(mine, -wi * seg, 0.0))
-
     pl.when(has_w)(tx_copy().wait_recv)
     pl.when(has_s)(ty_copy().wait_recv)
     for x in range(cx):
@@ -270,17 +288,37 @@
         coef[C_D, x] = inv * wz
         coef[C_U, x] = jnp.where(lane == cz - 1, 0.0, inv * ez)
         coef[C_INV, x] = inv
-        right = inv * rhs_ref[x]
-        coef[C_RHS, x] = right
-        p_buf[1, x] = right - inv * well_term[x * cy : (x + 1) * cy]
+        coef[C_RHS, x] = inv * rhs_ref[x]
+
+    for d in range(1, reach):
+        pack_copy(d).wait_recv()
+    for r in range(reach):
+        for k in range(4):
+            params[k, r * wells : (r + 1) * wells] = packs[r, k * wells : (k + 1) * wells]
+    host = params[0]
+    wi = params[1]
+    rate = params[3]
+    slot = lax.broadcasted_iota(jnp.int32, (rows, cz), 1)
+    fm = jnp.where(slot > 0, params[2], 0.0)
+    fp = jnp.where(slot < cz - 1, pltpu.roll(fm, cz - 1, 1), 0.0)
+    seg_inv = 0.8 / (wi + fm + fp)
+    mine = host == level
+
+    seg = seg_inv * rate
+    well_term = scatter(jnp.where(mine, -wi * seg, 0.0))
+    for x in range(cx):
+        p_buf[1, x] = coef[C_RHS, x] - coef[C_INV, x] * well_term[x * cy : (x + 1) * cy]
     send_halos(1)
 
     def sweep(t, seg, first):
         cell_p = gather(t)
+        cell_buf[t] = cell_p
+        for d in offsets:
+            cell_copy(t, d).start()
         if not first:
-            seg = merge(t - 1, seg)
-        seg = well_step(t, seg, cell_p)
-        well_term = scatter(jnp.where(mine, wi * (cell_p - seg), 0.0))
+            seg = well_step(seg, merge(t - 1))
+        flux = wi * (cell_p - well_step(seg, cell_p))
+        well_term = scatter(jnp.where(mine, flux, 0.0))
         return seg, well_term
 
     def middle(t, seg, first):
@@ -294,7 +332,7 @@
     last = SWEEPS - 1
     seg, well_term = sweep(last, seg, False)
     grid_step(last, well_term, p_out, None)
-    seg = merge(last, seg)
+    seg = well_step(seg, merge(last))
     s_out[0] = seg[:wells]
 
     for d in range(1, reach):
@@ -306,13 +344,14 @@
         for there, copy in halo_copies(t):
             pl.when(there)(copy.wait_send)
         for d in offsets:
-            seg_copy(t, d).wait_send()
+            cell_copy(t, d).wait_send()
         return carry
 
     lax.fori_loop(1, SWEEPS, drain, 0)
 
 
-def shards(rhs, acc, tx, ty, tz, held, host, wi, sc, sr):
+def shards(*args):
+    rhs, acc, tx, ty, tz, held, host, wi, sc, sr = args
     reach = held.shape[0]
     wells, slots = wi.shape[1:]
     rows = reach * wells
@@ -326,9 +365,11 @@
             jax.ShapeDtypeStruct(rhs.shape, f32),
             jax.ShapeDtypeStruct(sr.shape, f32),
         ),
-        in_specs=[vmem] * 10,
+        in_specs=[pl.BlockSpec(memory_space=pltpu.HBM)] * 10,
         out_specs=(vmem, vmem),
-        scratch_shapes=[
+        scratch_shapes=[pltpu.VMEM(a.shape, a.dtype) for a in args]
+        + [
+            pltpu.SemaphoreType.DMA((len(args),)),
             pltpu.VMEM((SWEEPS, cx, cy, cz), f32),
             pltpu.VMEM((SWEEPS, 4, cy, cz), f32),
             pltpu.VMEM((SWEEPS, 2, cx, cz), f32),
@@ -350,9 +391,9 @@
             pltpu.SemaphoreType.DMA((SWEEPS, peers)),
         ],
         compiler_params=pltpu.CompilerParams(
-            collective_id=0, has_side_effects=True, vmem_limit_bytes=32 * 1024 * 1024
+            collective_id=0, has_side_effects=True, vmem_limit_bytes=60 * 1024 * 1024
         ),
-    )(rhs, acc, tx, ty, tz, held, host, wi, sc, sr)
+    )(*args)
 
 
 def solution(mesh):

time: 40.2 us -> 30.1 us (0.75)
  local copies, waits for them, and re-layouts: 8.36 us -> 1.94 us
  Pallas kernels: 30.6 us -> 27.2 us
    unnamed x22 -> x4, local copies, waits for them, and re-layouts: 8.36 us -> 1.94 us
    pallas_call x1, Pallas kernels: 30.6 us -> 27.2 us  [shards(): pl.pallas_call(functools.partial(kernel, reach), out_shape=(jax.ShapeDtyp...]
where the time goes in v1:
time: 30.1 us; the launch traced here: 29.8 us
  Pallas kernels  27.2 us (90%)
  local copies, waits for them, and re-layouts  1.94 us (6%)
  between operations  0.65 us (2%)
    pallas_call x1, Pallas kernels, shards(): pl.pallas_call(functools.partial(kernel, reach), out_shape=(jax.ShapeDtyp...  27.2 us
    unnamed x4, local copies, waits for them, and re-layouts  1.94 us

profile of v1, /device:TPU:0, one launch (start us, length us, event | category | flops | bytes accessed | tf_op | source)
XLA Modules:
  0.0 29.8 jit_solution(11922075073490941285)
XLA Ops:
  0.6 27.2 %shard_map.113 = (f32[8,8,128]{2,1,0:T(8,128)}, f32[1,2,128]{2,1,0:T(2,128)}) custom-call(f32[8,8,128]{2,1,0:T(8,128)} %rhs_hbm.1, f32[8,8,128]{2,1,0:T(8,128)} %acc_hbm.1, f32[8,8,128]{2,1,0:T(8,128)} %tx_hbm.1, f32[8,8,128]{2,1,0:T(8,128)} %ty_hbm.1, f32[8,8,128]{2,1,0:T(8,128)} %tz_hbm.1, s32[4,1,2,128]{3,2,1,0:T(2,128)} %held_hbm.1, ...), custom_call_target="tpu_custom_call" | custom-call | tf_op jit(solution)/shard_map/pallas_call | solution.py:362
  27.8 0.0 copy-start
  27.9 1.4 %copy.14 = f32[8,8,128]{2,1,0:T(8,128)} copy(f32[8,8,128]{2,1,0:T(8,128)} %get-tuple-element.4) | data formatting | bytes 65536
  29.2 0.0 copy-done
  29.2 0.6 %copy.15 = f32[1,2,128]{2,1,0:T(2,128)} copy(f32[1,2,128]{2,1,0:T(2,128)S(1)} %copy-done) | data formatting | bytes 2048
Async XLA Ops:
  27.8 1.4 %copy-start = (f32[1,2,128]{2,1,0:T(2,128)S(1)}, f32[1,2,128]{2,1,0:T(2,128)}, u32[]{:S(2)}) copy-start(f32[1,2,128]{2,1,0:T(2,128)} %get-tuple-element.5) | copy-start | bytes 3076

commit v2 on v1

--- a/solution.py
+++ b/solution.py
@@ -48,7 +48,7 @@
     packs,
     params,
     held_buf,
-    slot_z,
+    slot_column,
     cell_buf,
     cell_recv,
     init_send,
@@ -158,11 +158,16 @@
     held = held_buf[...]
     row_of = held // cz
     z_of = held - row_of * cz
-    z_iota = lax.broadcasted_iota(jnp.int32, (cz, cz), 0)
+    lines = cx * cy // 2
+    half_of = row_of // lines
+    line_of = row_of - half_of * lines
+    column_of = half_of * cz + z_of
+    column_iota = lax.broadcasted_iota(jnp.int32, (2 * cz, cz), 0)
     for s in range(rows):
-        hit = (z_iota == jnp.broadcast_to(z_of[s : s + 1, :], (cz, cz))).astype(jnp.float32)
-        slot_z[s * cz : (s + 1) * cz, :] = hit.T.astype(jnp.bfloat16)
-    row_iota = lax.broadcasted_iota(jnp.int32, (cx * cy, cz), 0)
+        column = jnp.broadcast_to(column_of[s : s + 1, :], column_iota.shape)
+        hit = (column_iota == column).astype(jnp.float32)
+        slot_column[s * cz : (s + 1) * cz, :] = hit.T.astype(jnp.bfloat16)
+    line_iota = lax.broadcasted_iota(jnp.int32, (lines, cz), 0)
 
     lane = lax.broadcasted_iota(jnp.int32, (cy, cz), 1)
     sub = lax.broadcasted_iota(jnp.int32, (cy, cz), 0)
@@ -186,20 +191,25 @@
         rest = flux - high
         mid = rest.astype(jnp.bfloat16).astype(jnp.float32)
         low = rest - mid
-        parts = []
-        for part in (high, mid, low):
-            pieces = []
-            for s in range(rows):
-                at_row = row_iota == jnp.broadcast_to(row_of[s : s + 1, :], row_iota.shape)
-                pieces.append(
-                    jnp.where(at_row, jnp.broadcast_to(part[s : s + 1, :], row_iota.shape), 0.0)
-                )
-            parts.append(jnp.concatenate(pieces, axis=1).astype(jnp.bfloat16))
+        pieces = []
+        for s in range(rows):
+            at_line = line_iota == jnp.broadcast_to(line_of[s : s + 1, :], line_iota.shape)
+            pieces.append(
+                jnp.concatenate(
+                    [
+                        jnp.where(at_line, jnp.broadcast_to(part[s : s + 1, :], at_line.shape), 0.0)
+                        for part in (high, mid, low)
+                    ],
+                    axis=0,
+                ).astype(jnp.bfloat16)
+            )
         spread = jnp.dot(
-            jnp.concatenate(parts, axis=0), slot_z[...], preferred_element_type=jnp.float32
-        )
-        cells = cx * cy
-        return spread[:cells] + spread[cells : 2 * cells] + spread[2 * cells :]
+            jnp.concatenate(pieces, axis=1), slot_column[...], preferred_element_type=jnp.float32
+        )
+        spread = spread[:lines] + spread[lines : 2 * lines] + spread[2 * lines :]
+        return [
+            spread[x % (cx // 2) * cy :][:cy, x // (cx // 2) * cz :][:, :cz] for x in range(cx)
+        ]
 
     def halo_copies(t):
         return (
@@ -213,10 +223,14 @@
                          halo_recv.at[t, SOUTH], {"gy": gy + 1})),
         )
 
-    def send_halos(t):
+    def send_x(t):
+        for there, copy in halo_copies(t)[:2]:
+            pl.when(there)(copy.start)
+
+    def send_y(t):
         y_stage[t, 0] = p_buf[t, :, 0, :]
         y_stage[t, 1] = p_buf[t, :, cy - 1, :]
-        for there, copy in halo_copies(t):
+        for there, copy in halo_copies(t)[2:]:
             pl.when(there)(copy.start)
 
     def wait_halos(t):
@@ -247,7 +261,7 @@
         parts = []
         for x in range(cx):
             p = p_buf[t, x]
-            total = 0.3 * p + coef[C_RHS, x] - coef[C_INV, x] * well_term[x * cy : (x + 1) * cy]
+            total = 0.3 * p + coef[C_RHS, x] - coef[C_INV, x] * well_term[x]
             total += coef[C_U, x] * pltpu.roll(p, cz - 1, 1) + coef[C_D, x] * pltpu.roll(p, 1, 1)
             total += coef[C_N, x] * pltpu.roll(p, cy - 1, 0) + coef[C_S, x] * pltpu.roll(p, 1, 0)
             if x > 0:
@@ -258,7 +272,7 @@
         wait_halos(t)
         parts[0] += coef[C_W, 0] * halo[t, WEST]
         parts[-1] += coef[C_E, cx - 1] * halo[t, EAST]
-        for x in range(cx):
+        for place, x in enumerate([0, cx - 1] + list(range(1, cx - 1))):
             north = jnp.broadcast_to(halo[t, NORTH, pl.ds(x, 1), :], (cy, cz))
             south = jnp.broadcast_to(halo[t, SOUTH, pl.ds(x, 1), :], (cy, cz))
             edge = jnp.where(sub == 0, south, north)
@@ -267,6 +281,10 @@
                 result[x] = value
             else:
                 result[at, x] = value
+                if place == 1:
+                    send_x(at)
+        if at is not None:
+            send_y(at)
 
     pl.when(has_w)(tx_copy().wait_recv)
     pl.when(has_s)(ty_copy().wait_recv)
@@ -307,8 +325,9 @@
     seg = seg_inv * rate
     well_term = scatter(jnp.where(mine, -wi * seg, 0.0))
     for x in range(cx):
-        p_buf[1, x] = coef[C_RHS, x] - coef[C_INV, x] * well_term[x * cy : (x + 1) * cy]
-    send_halos(1)
+        p_buf[1, x] = coef[C_RHS, x] - coef[C_INV, x] * well_term[x]
+    send_x(1)
+    send_y(1)
 
     def sweep(t, seg, first):
         cell_p = gather(t)
@@ -324,7 +343,6 @@
     def middle(t, seg, first):
         seg, well_term = sweep(t, seg, first)
         grid_step(t, well_term, p_buf, t + 1)
-        send_halos(t + 1)
         return seg
 
     seg = middle(1, seg, True)
@@ -380,7 +398,7 @@
             pltpu.VMEM((reach, 4 * wells, slots), f32),
             pltpu.VMEM((4, rows, slots), f32),
             pltpu.VMEM((rows, slots), jnp.int32),
-            pltpu.VMEM((rows * slots, cz), jnp.bfloat16),
+            pltpu.VMEM((rows * slots, 2 * cz), jnp.bfloat16),
             pltpu.VMEM((SWEEPS, rows, slots), f32),
             pltpu.VMEM((SWEEPS, peers, rows, slots), f32),
             pltpu.SemaphoreType.DMA((reach + 1,)),

time: 30.1 us -> 30 us (level)
  no operation moved by 1% of the time
where the time goes in v2:
time: 30 us; the launch traced here: 29.8 us
  Pallas kernels  27.2 us (91%)
  local copies, waits for them, and re-layouts  1.94 us (6%)
  between operations  0.65 us (2%)
    pallas_call x1, Pallas kernels, shards(): pl.pallas_call(functools.partial(kernel, reach), out_shape=(jax.ShapeDtyp...  27.2 us
    unnamed x4, local copies, waits for them, and re-layouts  1.94 us

profile of v2, /device:TPU:0, one launch (start us, length us, event | category | flops | bytes accessed | tf_op | source)
XLA Modules:
  0.0 29.8 jit_solution(14960095847694710325)
XLA Ops:
  0.6 27.2 %shard_map.113 = (f32[8,8,128]{2,1,0:T(8,128)}, f32[1,2,128]{2,1,0:T(2,128)}) custom-call(f32[8,8,128]{2,1,0:T(8,128)} %rhs_hbm.1, f32[8,8,128]{2,1,0:T(8,128)} %acc_hbm.1, f32[8,8,128]{2,1,0:T(8,128)} %tx_hbm.1, f32[8,8,128]{2,1,0:T(8,128)} %ty_hbm.1, f32[8,8,128]{2,1,0:T(8,128)} %tz_hbm.1, s32[4,1,2,128]{3,2,1,0:T(2,128)} %held_hbm.1, ...), custom_call_target="tpu_custom_call" | custom-call | tf_op jit(solution)/shard_map/pallas_call | solution.py:380
  27.8 0.0 copy-start
  27.8 1.4 %copy.14 = f32[8,8,128]{2,1,0:T(8,128)} copy(f32[8,8,128]{2,1,0:T(8,128)} %get-tuple-element.4) | data formatting | bytes 65536
  29.2 0.0 copy-done
  29.2 0.6 %copy.15 = f32[1,2,128]{2,1,0:T(2,128)} copy(f32[1,2,128]{2,1,0:T(2,128)S(1)} %copy-done) | data formatting | bytes 2048
Async XLA Ops:
  27.8 1.4 %copy-start = (f32[1,2,128]{2,1,0:T(2,128)S(1)}, f32[1,2,128]{2,1,0:T(2,128)}, u32[]{:S(2)}) copy-start(f32[1,2,128]{2,1,0:T(2,128)} %get-tuple-element.5) | copy-start | bytes 3076

commit v3 on v2

--- a/solution.py
+++ b/solution.py
@@ -25,8 +25,8 @@
     wi_hbm,
     sc_hbm,
     sr_hbm,
-    p_out,
-    s_out,
+    p_hbm,
+    s_hbm,
     rhs_ref,
     acc_ref,
     tx_ref,
@@ -38,6 +38,8 @@
     sc_ref,
     sr_ref,
     fetch_sem,
+    s_out,
+    out_sem,
     p_buf,
     halo,
     y_stage,
@@ -233,20 +235,27 @@
         for there, copy in halo_copies(t)[2:]:
             pl.when(there)(copy.start)
 
-    def wait_halos(t):
-        for there, slot_at in ((has_w, WEST), (has_e, EAST), (has_s, SOUTH), (has_n, NORTH)):
-            copy = send(halo.at[t, slot_at], halo.at[t, slot_at], halo_send.at[t, slot_at],
-                        halo_recv.at[t, slot_at], along_x(1))
-            pl.when(there)(copy.wait_recv)
+    def wait_halo(t, side):
+        there = (has_w, has_e, has_s, has_n)[side]
+        copy = send(halo.at[t, side], halo.at[t, side], halo_send.at[t, side],
+                    halo_recv.at[t, side], along_x(1))
+        pl.when(there)(copy.wait_recv)
+
+    def all_cells(t):
+        return send(cell_recv.at[t], cell_recv.at[t], cell_send.at[t], cell_rsem.at[t], along_x(1))
+
+    def drain(t):
+        for there, copy in halo_copies(t):
+            pl.when(there)(copy.wait_send)
+        all_cells(t).wait_send()
 
     def cell_copy(t, d):
         return send(cell_buf.at[t], cell_recv.at[t, index_of[-d]],
-                    cell_send.at[t, index_of[d]], cell_rsem.at[t, index_of[-d]], along_x(d))
+                    cell_send.at[t], cell_rsem.at[t], along_x(d))
 
     def merge(t):
         cell_p = cell_buf[t]
-        for d in offsets:
-            cell_copy(t, d).wait_recv()
+        all_cells(t).wait_recv()
         for d in offsets:
             got = pltpu.roll(cell_recv[t, index_of[d]], (-d * wells) % rows, 0)
             cell_p = jnp.where(host == level + d, got, cell_p)
@@ -257,7 +266,7 @@
         after = pltpu.roll(seg, cz - 1, 1)
         return 0.2 * seg + seg_inv * (rate + wi * cell_p + fm * before + fp * after)
 
-    def grid_step(t, well_term, result, at):
+    def grid_step(t, well_term, more):
         parts = []
         for x in range(cx):
             p = p_buf[t, x]
@@ -269,22 +278,22 @@
             if x < cx - 1:
                 total += coef[C_E, x] * p_buf[t, x + 1]
             parts.append(total)
-        wait_halos(t)
-        parts[0] += coef[C_W, 0] * halo[t, WEST]
-        parts[-1] += coef[C_E, cx - 1] * halo[t, EAST]
-        for place, x in enumerate([0, cx - 1] + list(range(1, cx - 1))):
+        wait_halo(t, SOUTH)
+        wait_halo(t, NORTH)
+        for x in range(cx):
             north = jnp.broadcast_to(halo[t, NORTH, pl.ds(x, 1), :], (cy, cz))
             south = jnp.broadcast_to(halo[t, SOUTH, pl.ds(x, 1), :], (cy, cz))
-            edge = jnp.where(sub == 0, south, north)
-            value = parts[x] + coef[C_EDGE, x] * edge
-            if at is None:
-                result[x] = value
-            else:
-                result[at, x] = value
-                if place == 1:
-                    send_x(at)
-        if at is not None:
-            send_y(at)
+            parts[x] += coef[C_EDGE, x] * jnp.where(sub == 0, south, north)
+            if 0 < x < cx - 1:
+                p_buf[t + 1, x] = parts[x]
+        copies = halo_copies(t + 1) if more else None
+        for side, x, at in ((WEST, 0, C_W), (EAST, cx - 1, C_E)):
+            wait_halo(t, side)
+            p_buf[t + 1, x] = parts[x] + coef[at, x] * halo[t, side]
+            if more:
+                pl.when(copies[side][0])(copies[side][1].start)
+        if more:
+            send_y(t + 1)
 
     pl.when(has_w)(tx_copy().wait_recv)
     pl.when(has_s)(ty_copy().wait_recv)
@@ -342,30 +351,30 @@
 
     def middle(t, seg, first):
         seg, well_term = sweep(t, seg, first)
-        grid_step(t, well_term, p_buf, t + 1)
+        if not first:
+            drain(t - 1)
+        grid_step(t, well_term, True)
         return seg
 
     seg = middle(1, seg, True)
     seg = lax.fori_loop(2, SWEEPS - 1, lambda t, seg: middle(t, seg, False), seg)
     last = SWEEPS - 1
     seg, well_term = sweep(last, seg, False)
-    grid_step(last, well_term, p_out, None)
-    seg = well_step(seg, merge(last))
-    s_out[0] = seg[:wells]
-
+    drain(last - 1)
+    grid_step(last, well_term, False)
+    p_copy = pltpu.make_async_copy(p_buf.at[SWEEPS], p_hbm, out_sem.at[0])
+    p_copy.start()
     for d in range(1, reach):
         pack_copy(d).wait_send()
     pl.when(has_e)(lambda: tx_copy().wait_send())
     pl.when(has_n)(lambda: ty_copy().wait_send())
-
-    def drain(t, carry):
-        for there, copy in halo_copies(t):
-            pl.when(there)(copy.wait_send)
-        for d in offsets:
-            cell_copy(t, d).wait_send()
-        return carry
-
-    lax.fori_loop(1, SWEEPS, drain, 0)
+    drain(last)
+    seg = well_step(seg, merge(last))
+    s_out[0] = seg[:wells]
+    s_copy = pltpu.make_async_copy(s_out, s_hbm, out_sem.at[1])
+    s_copy.start()
+    p_copy.wait()
+    s_copy.wait()
 
 
 def shards(*args):
@@ -375,7 +384,7 @@
     rows = reach * wells
     cx, cy, cz = rhs.shape
     peers = 2 * (reach - 1)
-    vmem = pl.BlockSpec(memory_space=pltpu.VMEM)
+    hbm = pl.BlockSpec(memory_space=pltpu.HBM)
     f32 = jnp.float32
     return pl.pallas_call(
         functools.partial(kernel, reach),
@@ -383,12 +392,14 @@
             jax.ShapeDtypeStruct(rhs.shape, f32),
             jax.ShapeDtypeStruct(sr.shape, f32),
         ),
-        in_specs=[pl.BlockSpec(memory_space=pltpu.HBM)] * 10,
-        out_specs=(vmem, vmem),
+        in_specs=[hbm] * 10,
+        out_specs=(hbm, hbm),
         scratch_shapes=[pltpu.VMEM(a.shape, a.dtype) for a in args]
         + [
             pltpu.SemaphoreType.DMA((len(args),)),
-            pltpu.VMEM((SWEEPS, cx, cy, cz), f32),
+            pltpu.VMEM(sr.shape, f32),
+            pltpu.SemaphoreType.DMA((2,)),
+            pltpu.VMEM((SWEEPS + 1, cx, cy, cz), f32),
             pltpu.VMEM((SWEEPS, 4, cy, cz), f32),
             pltpu.VMEM((SWEEPS, 2, cx, cz), f32),
             pltpu.VMEM((9, cx, cy, cz), f32),
@@ -405,8 +416,8 @@
             pltpu.SemaphoreType.DMA((reach + 1,)),
             pltpu.SemaphoreType.DMA((SWEEPS, 4)),
             pltpu.SemaphoreType.DMA((SWEEPS, 4)),
-            pltpu.SemaphoreType.DMA((SWEEPS, peers)),
-            pltpu.SemaphoreType.DMA((SWEEPS, peers)),
+            pltpu.SemaphoreType.DMA((SWEEPS,)),
+            pltpu.SemaphoreType.DMA((SWEEPS,)),
         ],
         compiler_params=pltpu.CompilerParams(
             collective_id=0, has_side_effects=True, vmem_limit_bytes=60 * 1024 * 1024

time: 30 us -> 29.3 us (0.977)
  Pallas kernels: 27.2 us -> 26.4 us
    pallas_call x1, Pallas kernels: 27.2 us -> 26.4 us  [shards(): pl.pallas_call(functools.partial(kernel, reach), out_shape=(jax.ShapeDtyp...]
where the time goes in v3:
time: 29.3 us; the launch traced here: 29 us
  Pallas kernels  26.4 us (90%)
  local copies, waits for them, and re-layouts  1.94 us (7%)
  between operations  0.65 us (2%)
    pallas_call x1, Pallas kernels, shards(): pl.pallas_call(functools.partial(kernel, reach), out_shape=(jax.ShapeDtyp...  26.4 us
    unnamed x4, local copies, waits for them, and re-layouts  1.94 us

profile of v3, /device:TPU:0, one launch (start us, length us, event | category | flops | bytes accessed | tf_op | source)
XLA Modules:
  0.0 29.0 jit_solution(791059600050546838)
XLA Ops:
  0.6 26.4 %shard_map.113 = (f32[8,8,128]{2,1,0:T(8,128)}, f32[1,2,128]{2,1,0:T(2,128)}) custom-call(f32[8,8,128]{2,1,0:T(8,128)} %rhs_hbm.1, f32[8,8,128]{2,1,0:T(8,128)} %acc_hbm.1, f32[8,8,128]{2,1,0:T(8,128)} %tx_hbm.1, f32[8,8,128]{2,1,0:T(8,128)} %ty_hbm.1, f32[8,8,128]{2,1,0:T(8,128)} %tz_hbm.1, s32[4,1,2,128]{3,2,1,0:T(2,128)} %held_hbm.1, ...), custom_call_target="tpu_custom_call" | custom-call | tf_op jit(solution)/shard_map/pallas_call | solution.py:389
  27.1 0.0 copy-start
  27.1 1.4 %copy.14 = f32[8,8,128]{2,1,0:T(8,128)} copy(f32[8,8,128]{2,1,0:T(8,128)} %get-tuple-element.4) | data formatting | bytes 65536
  28.5 0.0 copy-done
  28.5 0.6 %copy.15 = f32[1,2,128]{2,1,0:T(2,128)} copy(f32[1,2,128]{2,1,0:T(2,128)S(1)} %copy-done) | data formatting | bytes 2048
Async XLA Ops:
  27.1 1.4 %copy-start = (f32[1,2,128]{2,1,0:T(2,128)S(1)}, f32[1,2,128]{2,1,0:T(2,128)}, u32[]{:S(2)}) copy-start(f32[1,2,128]{2,1,0:T(2,128)} %get-tuple-element.5) | copy-start | bytes 3076

commit v4 on v3

--- a/solution.py
+++ b/solution.py
@@ -83,10 +83,21 @@
             device_id_type=MESH,
         )
 
+    def partner(axis, at, other, at_other, step, there):
+        inside = there.astype(jnp.int32)
+        return {
+            axis: at + step * inside,
+            other: at_other + (1 - inside) * (1 - 2 * lax.rem(at_other, 2)),
+        }
+
+    partners = (
+        partner("gx", gx, "gy", gy, -1, has_w),
+        partner("gx", gx, "gy", gy, 1, has_e),
+        partner("gy", gy, "gx", gx, -1, has_s),
+        partner("gy", gy, "gx", gx, 1, has_n),
+    )
+
     zero = jnp.zeros((cy, cz), jnp.float32)
-    for t in range(SWEEPS):
-        for side in range(4):
-            halo[t, side] = zero
     tx_halo[...] = zero
     ty_halo[...] = zero
 
@@ -94,13 +105,8 @@
     for d in offsets:
         pl.semaphore_signal(barrier, inc=1, device_id=along_x(d), device_id_type=MESH)
 
-    @pl.when(has_s)
-    def _():
-        pl.semaphore_signal(barrier, inc=1, device_id={"gy": gy - 1}, device_id_type=MESH)
-
-    @pl.when(has_n)
-    def _():
-        pl.semaphore_signal(barrier, inc=1, device_id={"gy": gy + 1}, device_id_type=MESH)
+    for device in partners:
+        pl.semaphore_signal(barrier, inc=1, device_id=device, device_id_type=MESH)
 
     fetches = [
         pltpu.make_async_copy(src, dst, fetch_sem.at[i])
@@ -128,9 +134,7 @@
     packs[0, 2 * wells : 3 * wells] = sc_ref[0]
     packs[0, 3 * wells : 4 * wells] = sr_ref[0]
     ty_stage[...] = ty_ref[:, cy - 1, :]
-    pl.semaphore_wait(
-        barrier, len(offsets) + has_s.astype(jnp.int32) + has_n.astype(jnp.int32)
-    )
+    pl.semaphore_wait(barrier, len(offsets) + len(partners))
 
     def pack_copy(d):
         return send(
@@ -213,40 +217,33 @@
             spread[x % (cx // 2) * cy :][:cy, x // (cx // 2) * cz :][:, :cz] for x in range(cx)
         ]
 
-    def halo_copies(t):
-        return (
-            (has_w, send(p_buf.at[t, 0], halo.at[t, EAST], halo_send.at[t, WEST],
-                         halo_recv.at[t, EAST], {"gx": gx - 1})),
-            (has_e, send(p_buf.at[t, cx - 1], halo.at[t, WEST], halo_send.at[t, EAST],
-                         halo_recv.at[t, WEST], {"gx": gx + 1})),
-            (has_s, send(y_stage.at[t, 0], halo.at[t, NORTH], halo_send.at[t, SOUTH],
-                         halo_recv.at[t, NORTH], {"gy": gy - 1})),
-            (has_n, send(y_stage.at[t, 1], halo.at[t, SOUTH], halo_send.at[t, NORTH],
-                         halo_recv.at[t, SOUTH], {"gy": gy + 1})),
-        )
+    def halo_copy(t, side):
+        src = (p_buf.at[t, 0], p_buf.at[t, cx - 1], y_stage.at[t, 0], y_stage.at[t, 1])[side]
+        there = (has_w, has_e, has_s, has_n)[side].astype(jnp.int32)
+        opposite = (EAST, WEST, NORTH, SOUTH)[side]
+        lands = side + (opposite - side) * there
+        return send(src, halo.at[t, lands], halo_send.at[t], halo_recv.at[t, lands],
+                    partners[side])
 
     def send_x(t):
-        for there, copy in halo_copies(t)[:2]:
-            pl.when(there)(copy.start)
+        halo_copy(t, WEST).start()
+        halo_copy(t, EAST).start()
 
     def send_y(t):
         y_stage[t, 0] = p_buf[t, :, 0, :]
         y_stage[t, 1] = p_buf[t, :, cy - 1, :]
-        for there, copy in halo_copies(t)[2:]:
-            pl.when(there)(copy.start)
+        halo_copy(t, SOUTH).start()
+        halo_copy(t, NORTH).start()
 
     def wait_halo(t, side):
-        there = (has_w, has_e, has_s, has_n)[side]
-        copy = send(halo.at[t, side], halo.at[t, side], halo_send.at[t, side],
-                    halo_recv.at[t, side], along_x(1))
-        pl.when(there)(copy.wait_recv)
+        send(halo.at[t, side], halo.at[t, side], halo_send.at[t],
+             halo_recv.at[t, side], partners[side]).wait_recv()
 
     def all_cells(t):
         return send(cell_recv.at[t], cell_recv.at[t], cell_send.at[t], cell_rsem.at[t], along_x(1))
 
     def drain(t):
-        for there, copy in halo_copies(t):
-            pl.when(there)(copy.wait_send)
+        send(halo.at[t], halo.at[t], halo_send.at[t], halo_recv.at[t, 0], partners[0]).wait_send()
         all_cells(t).wait_send()
 
     def cell_copy(t, d):
@@ -286,12 +283,11 @@
             parts[x] += coef[C_EDGE, x] * jnp.where(sub == 0, south, north)
             if 0 < x < cx - 1:
                 p_buf[t + 1, x] = parts[x]
-        copies = halo_copies(t + 1) if more else None
         for side, x, at in ((WEST, 0, C_W), (EAST, cx - 1, C_E)):
             wait_halo(t, side)
             p_buf[t + 1, x] = parts[x] + coef[at, x] * halo[t, side]
             if more:
-                pl.when(copies[side][0])(copies[side][1].start)
+                halo_copy(t + 1, side).start()
         if more:
             send_y(t + 1)
 
@@ -306,11 +302,11 @@
         diag = acc_ref[x] + ex + wx + ey + wy + ez + wz
         inv = 0.7 / diag
         coef[C_W, x] = inv * wx
-        coef[C_E, x] = inv * ex
+        coef[C_E, x] = jnp.where(has_e, inv * ex, 0.0) if x == cx - 1 else inv * ex
         coef[C_S, x] = jnp.where(sub == 0, 0.0, inv * wy)
         coef[C_N, x] = jnp.where(sub == cy - 1, 0.0, inv * ey)
         coef[C_EDGE, x] = jnp.where(
-            sub == 0, inv * wy, jnp.where(sub == cy - 1, inv * ey, 0.0)
+            sub == 0, inv * wy, jnp.where((sub == cy - 1) & has_n, inv * ey, 0.0)
         )
         coef[C_D, x] = inv * wz
         coef[C_U, x] = jnp.where(lane == cz - 1, 0.0, inv * ez)
@@ -377,6 +373,17 @@
     s_copy.wait()
 
 
+def hand_out(p_in, s_in, p_out, s_out, sems):
+    copies = (
+        pltpu.make_async_copy(p_in, p_out, sems.at[0]),
+        pltpu.make_async_copy(s_in, s_out, sems.at[1]),
+    )
+    for copy in copies:
+        copy.start()
+    for copy in copies:
+        copy.wait()
+
+
 def shards(*args):
     rhs, acc, tx, ty, tz, held, host, wi, sc, sr = args
     reach = held.shape[0]
@@ -386,12 +393,10 @@
     peers = 2 * (reach - 1)
     hbm = pl.BlockSpec(memory_space=pltpu.HBM)
     f32 = jnp.float32
-    return pl.pallas_call(
+    shapes = (jax.ShapeDtypeStruct(rhs.shape, f32), jax.ShapeDtypeStruct(sr.shape, f32))
+    swept = pl.pallas_call(
         functools.partial(kernel, reach),
-        out_shape=(
-            jax.ShapeDtypeStruct(rhs.shape, f32),
-            jax.ShapeDtypeStruct(sr.shape, f32),
-        ),
+        out_shape=shapes,
         in_specs=[hbm] * 10,
         out_specs=(hbm, hbm),
         scratch_shapes=[pltpu.VMEM(a.shape, a.dtype) for a in args]
@@ -414,7 +419,7 @@
             pltpu.VMEM((SWEEPS, peers, rows, slots), f32),
             pltpu.SemaphoreType.DMA((reach + 1,)),
             pltpu.SemaphoreType.DMA((reach + 1,)),
-            pltpu.SemaphoreType.DMA((SWEEPS, 4)),
+            pltpu.SemaphoreType.DMA((SWEEPS,)),
             pltpu.SemaphoreType.DMA((SWEEPS, 4)),
             pltpu.SemaphoreType.DMA((SWEEPS,)),
             pltpu.SemaphoreType.DMA((SWEEPS,)),
@@ -423,6 +428,14 @@
             collective_id=0, has_side_effects=True, vmem_limit_bytes=60 * 1024 * 1024
         ),
     )(*args)
+    return pl.pallas_call(
+        hand_out,
+        out_shape=shapes,
+        in_specs=[hbm] * 2,
+        out_specs=(hbm, hbm),
+        scratch_shapes=[pltpu.SemaphoreType.DMA((2,))],
+        compiler_params=pltpu.CompilerParams(vmem_limit_bytes=60 * 1024 * 1024),
+    )(*swept)
 
 
 def solution(mesh):

time: 29.3 us -> 29.3 us (level)
  Pallas kernels: 26.4 us -> 28.5 us
  local copies, waits for them, and re-layouts: 1.94 us -> 0 us
    pallas_call x1 -> x2, Pallas kernels: 26.4 us -> 28.5 us  [the longest x1 26.3 us: shards(): pl.pallas_call(functools.partial(kernel, reach), out_shape=shapes, in_spe...]
    unnamed x4 -> x0, local copies, waits for them, and re-layouts: 1.94 us -> none
where the time goes in v4:
time: 29.3 us; the launch traced here: 29.1 us
  Pallas kernels  28.5 us (97%)
  between operations  0.64 us (2%)
    pallas_call x1, Pallas kernels, shards(): pl.pallas_call(functools.partial(kernel, reach), out_shape=shapes, in_spe...  26.3 us
    pallas_call x1, Pallas kernels, shards(): pl.pallas_call(hand_out, out_shape=shapes, in_specs=[hbm] * 2, out_specs=...  2.14 us

profile of v4, /device:TPU:0, one launch (start us, length us, event | category | flops | bytes accessed | tf_op | source)
XLA Modules:
  0.0 29.1 jit_solution(8345053969440333492)
XLA Ops:
  0.6 26.3 %shard_map.113 = (f32[8,8,128]{2,1,0:T(8,128)}, f32[1,2,128]{2,1,0:T(2,128)}) custom-call(f32[8,8,128]{2,1,0:T(8,128)} %rhs_hbm.1, f32[8,8,128]{2,1,0:T(8,128)} %acc_hbm.1, f32[8,8,128]{2,1,0:T(8,128)} %tx_hbm.1, f32[8,8,128]{2,1,0:T(8,128)} %ty_hbm.1, f32[8,8,128]{2,1,0:T(8,128)} %tz_hbm.1, s32[4,1,2,128]{3,2,1,0:T(2,128)} %held_hbm.1, ...), custom_call_target="tpu_custom_call" | custom-call | tf_op jit(solution)/shard_map/pallas_call | solution.py:397
  27.0 2.1 %shard_map.114 = (f32[8,8,128]{2,1,0:T(8,128)}, f32[1,2,128]{2,1,0:T(2,128)}) custom-call(f32[8,8,128]{2,1,0:T(8,128)} %get-tuple-element.4.p_in, f32[1,2,128]{2,1,0:T(2,128)} %get-tuple-element.5.s_in), custom_call_target="tpu_custom_call" | custom-call | tf_op jit(solution)/shard_map/pallas_call | solution.py:431

commit v5 on v4

--- a/solution.py
+++ b/solution.py
@@ -373,14 +373,16 @@
     s_copy.wait()
 
 
-def hand_out(p_in, s_in, p_out, s_out, sems):
-    copies = (
-        pltpu.make_async_copy(p_in, p_out, sems.at[0]),
-        pltpu.make_async_copy(s_in, s_out, sems.at[1]),
-    )
-    for copy in copies:
+def hand_out(p_in, s_in, p_out, s_out, p_held, s_held, sems):
+    arrays = ((p_in, p_held, p_out), (s_in, s_held, s_out))
+    inward = [pltpu.make_async_copy(a, b, sems.at[0, i]) for i, (a, b, _) in enumerate(arrays)]
+    outward = [pltpu.make_async_copy(b, c, sems.at[1, i]) for i, (_, b, c) in enumerate(arrays)]
+    for copy in inward:
         copy.start()
-    for copy in copies:
+    for fetched, copy in zip(inward, outward):
+        fetched.wait()
+        copy.start()
+    for copy in outward:
         copy.wait()
 
 
@@ -433,7 +435,11 @@
         out_shape=shapes,
         in_specs=[hbm] * 2,
         out_specs=(hbm, hbm),
-        scratch_shapes=[pltpu.SemaphoreType.DMA((2,))],
+        scratch_shapes=[
+            pltpu.VMEM(rhs.shape, f32),
+            pltpu.VMEM(sr.shape, f32),
+            pltpu.SemaphoreType.DMA((2, 2)),
+        ],
         compiler_params=pltpu.CompilerParams(vmem_limit_bytes=60 * 1024 * 1024),
     )(*swept)
 

time: 29.3 us -> 28.6 us (0.976)
  Pallas kernels: 28.5 us -> 27.7 us
    pallas_call x1, Pallas kernels: 2.14 us -> 1.41 us  [shards(): pl.pallas_call(hand_out, out_shape=shapes, in_specs=[hbm] * 2, out_specs=...]
where the time goes in v5:
time: 28.6 us; the launch traced here: 28.4 us
  Pallas kernels  27.7 us (97%)
  between operations  0.64 us (2%)
    pallas_call x1, Pallas kernels, shards(): pl.pallas_call(functools.partial(kernel, reach), out_shape=shapes, in_spe...  26.3 us
    pallas_call x1, Pallas kernels, shards(): pl.pallas_call(hand_out, out_shape=shapes, in_specs=[hbm] * 2, out_specs=...  1.41 us

profile of v5, /device:TPU:0, one launch (start us, length us, event | category | flops | bytes accessed | tf_op | source)
XLA Modules:
  0.0 28.4 jit_solution(11935027763545913655)
XLA Ops:
  0.6 26.3 %shard_map.113 = (f32[8,8,128]{2,1,0:T(8,128)}, f32[1,2,128]{2,1,0:T(2,128)}) custom-call(f32[8,8,128]{2,1,0:T(8,128)} %rhs_hbm.1, f32[8,8,128]{2,1,0:T(8,128)} %acc_hbm.1, f32[8,8,128]{2,1,0:T(8,128)} %tx_hbm.1, f32[8,8,128]{2,1,0:T(8,128)} %ty_hbm.1, f32[8,8,128]{2,1,0:T(8,128)} %tz_hbm.1, s32[4,1,2,128]{3,2,1,0:T(2,128)} %held_hbm.1, ...), custom_call_target="tpu_custom_call" | custom-call | tf_op jit(solution)/shard_map/pallas_call | solution.py:399
  27.0 1.4 %shard_map.114 = (f32[8,8,128]{2,1,0:T(8,128)}, f32[1,2,128]{2,1,0:T(2,128)}) custom-call(f32[8,8,128]{2,1,0:T(8,128)} %get-tuple-element.4.p_in, f32[1,2,128]{2,1,0:T(2,128)} %get-tuple-element.5.s_in), custom_call_target="tpu_custom_call" | custom-call | tf_op jit(solution)/shard_map/pallas_call | solution.py:433

commit v6 on v5

--- a/solution.py
+++ b/solution.py
@@ -337,12 +337,12 @@
     def sweep(t, seg, first):
         cell_p = gather(t)
         cell_buf[t] = cell_p
-        for d in offsets:
-            cell_copy(t, d).start()
         if not first:
             seg = well_step(seg, merge(t - 1))
         flux = wi * (cell_p - well_step(seg, cell_p))
         well_term = scatter(jnp.where(mine, flux, 0.0))
+        for d in offsets:
+            cell_copy(t, d).start()
         return seg, well_term
 
     def middle(t, seg, first):

time: 28.6 us -> 33.1 us (1.16)
  Pallas kernels: 27.7 us -> 32.2 us
    pallas_call x1, Pallas kernels: 26.3 us -> 30.8 us  [shards(): pl.pallas_call(functools.partial(kernel, reach), out_shape=shapes, in_spe...]
where the time goes in v6:
time: 33.1 us; the launch traced here: 32.8 us
  Pallas kernels  32.2 us (97%)
  between operations  0.64 us (2%)
    pallas_call x1, Pallas kernels, shards(): pl.pallas_call(functools.partial(kernel, reach), out_shape=shapes, in_spe...  30.8 us
    pallas_call x1, Pallas kernels, shards(): pl.pallas_call(hand_out, out_shape=shapes, in_specs=[hbm] * 2, out_specs=...  1.41 us

profile of v6, /device:TPU:0, one launch (start us, length us, event | category | flops | bytes accessed | tf_op | source)
XLA Modules:
  0.0 32.8 jit_solution(12589978383943344834)
XLA Ops:
  0.6 30.8 %shard_map.113 = (f32[8,8,128]{2,1,0:T(8,128)}, f32[1,2,128]{2,1,0:T(2,128)}) custom-call(f32[8,8,128]{2,1,0:T(8,128)} %rhs_hbm.1, f32[8,8,128]{2,1,0:T(8,128)} %acc_hbm.1, f32[8,8,128]{2,1,0:T(8,128)} %tx_hbm.1, f32[8,8,128]{2,1,0:T(8,128)} %ty_hbm.1, f32[8,8,128]{2,1,0:T(8,128)} %tz_hbm.1, s32[4,1,2,128]{3,2,1,0:T(2,128)} %held_hbm.1, ...), custom_call_target="tpu_custom_call" | custom-call | tf_op jit(solution)/shard_map/pallas_call | solution.py:399
  31.4 1.4 %shard_map.114 = (f32[8,8,128]{2,1,0:T(8,128)}, f32[1,2,128]{2,1,0:T(2,128)}) custom-call(f32[8,8,128]{2,1,0:T(8,128)} %get-tuple-element.4.p_in, f32[1,2,128]{2,1,0:T(2,128)} %get-tuple-element.5.s_in), custom_call_target="tpu_custom_call" | custom-call | tf_op jit(solution)/shard_map/pallas_call | solution.py:433
